TPU v7x, 128 devices: a whole 4x4x4 slice. The times are simulated.
128 devices in a mesh: grp: 8 (over z, core), sp: 16 (over x, y).
Axes of the slice: x: 4, y: 4, z: 4, core: 2. Of those that a mesh axis runs over, the one named last changes fastest.
Arguments:
- queries: bfloat16 [16, 16, 256, 1536], P(None, None, ('grp', 'sp')), may hold values from -64 to 64
- key_rows: bfloat16 [16, 16, 256, 1536], P(None, None, ('grp', 'sp')), may hold values from -6 to 6
- values: bfloat16 [16, 16, 256, 1536], P(None, None, ('grp', 'sp')), may hold values from -6 to 6
- query_gain: float32 [128], replicated, may hold values from 0.3 to 4.5
- key_gain: float32 [128], replicated, may hold values from 0.3 to 4.5
- frames_per_clip: int32 [16], replicated, may hold values from 4 to 16, as said below
- latent_height: int32 [16], replicated, may hold values from 2 to 4, as said below
- latent_width: int32 [16], replicated, may hold values from 32 to 64, as said below
- clip_plan: int32 [8], replicated, may hold values from 0 to 15, as said below
Outputs:
- block_out: bfloat16 [8, 16, 256, 1536], P('grp', 'sp')
Inputs may be any that keep to these rules, and one draw needn't show every extreme that they name: `frames_per_clip`: at least a quarter of 16; some clip named by clip_plan has exactly 16 frames and also the largest height and width. `latent_height`: some clip named by clip_plan reaches 4. `latent_width`: some clip named by clip_plan reaches 64. `clip_plan`: distinct clips, one for each group.
All inputs are finite; a program needn't handle non-finite values.
Results may differ from a plain program's by a relative error of at most 0.0054.
Values may be sent and summed in bfloat16 or wider, within the bound.
A program may use at most 64 MiB of HBM per device.

v0:
```python
import jax
import jax.numpy as jnp
from jax import lax
from jax.sharding import PartitionSpec as P

HEAD_DIM = 128


def attend_frames(routed_queries, routed_keys, routed_values, frame_base, frame_limit, live_count):
    frame_local, spatial_len, row_width = routed_queries.shape
    head_count = row_width // HEAD_DIM
    score_scale = HEAD_DIM ** (-0.5)
    block_rows = 512
    while spatial_len % block_rows:
        block_rows = block_rows // 2
    positions = jnp.arange(spatial_len, dtype=jnp.int32)
    key_live = positions < live_count
    key_heads = routed_keys[0].reshape(spatial_len, head_count, HEAD_DIM)
    value_heads = routed_values[0].reshape(spatial_len, head_count, HEAD_DIM)
    frame_on = frame_base + 0 < frame_limit
    query_heads = routed_queries[0, 0:block_rows].reshape(block_rows, head_count, HEAD_DIM)
    scores = (
        jnp.einsum("qhd,khd->hqk", query_heads, key_heads, preferred_element_type=jnp.float32)
        * score_scale
    )
    scores = jnp.where(key_live[None, None, :], scores, -jnp.inf)
    maxima = jnp.max(scores, axis=-1, keepdims=True)
    weights = jnp.exp(scores - maxima)
    totals = jnp.sum(weights, axis=-1)
    rounded = weights.astype(jnp.bfloat16)
    mixed = jnp.einsum("hqk,khd->qhd", rounded, value_heads, preferred_element_type=jnp.float32)
    mixed = mixed / jnp.transpose(totals)[:, :, None]
    rows_live = (positions < live_count) & frame_on
    mixed = jnp.where(rows_live[:, None, None], mixed, jnp.float32(0.0))
    pieces = mixed.reshape(block_rows, row_width).astype(jnp.bfloat16)
    outputs = [pieces]
    return jnp.stack(outputs, axis=0)


def temporal_mix(arrived, query_gain, key_gain, frame_limit, live_count, first_position):
    score_scale = HEAD_DIM ** (-0.5)
    values32 = arrived.astype(jnp.float32)
    normed = values32 * lax.rsqrt(jnp.mean(values32 * values32, axis=-1, keepdims=True) + 1e-06)
    query_side = normed * query_gain
    key_side = normed * key_gain
    scores = (
        jnp.einsum("fshd,gshd->shfg", query_side, key_side, precision=lax.Precision.HIGHEST)
        * score_scale
    )
    frame_ids = jnp.arange(arrived.shape[0], dtype=jnp.int32)
    frames_live = frame_ids < frame_limit
    scores = jnp.where(frames_live[None, None, None, :], scores, -jnp.inf)
    maxima = jnp.max(scores, axis=-1, keepdims=True)
    weights = jnp.exp(scores - maxima)
    totals = jnp.sum(weights, axis=-1)
    rounded = weights.astype(jnp.bfloat16)
    mixed = jnp.einsum("shfg,gshd->fshd", rounded, arrived, preferred_element_type=jnp.float32)
    mixed = mixed / jnp.transpose(totals, (2, 0, 1))[..., None]
    positions = first_position + jnp.arange(arrived.shape[1], dtype=jnp.int32)
    rows_live = frames_live[:, None] & (positions < live_count)[None, :]
    mixed = jnp.where(rows_live[:, :, None, None], mixed, jnp.float32(0.0))
    return mixed.astype(jnp.bfloat16)


def on_device(
    queries,
    key_rows,
    values,
    query_gain,
    key_gain,
    frames_per_clip,
    latent_height,
    latent_width,
    clip_plan,
):
    group_index = lax.axis_index("grp")
    shard_index = lax.axis_index("sp")
    loaded_count, frame_total, slab_rows, row_width = queries.shape
    ordered = tuple((jnp.take(tensor, clip_plan, axis=0) for tensor in (queries, key_rows, values)))
    group_count = ordered[0].shape[0]
    flattened = tuple(
        (tensor.reshape(group_count * frame_total, slab_rows, row_width) for tensor in ordered)
    )
    routed = (
        lax.all_to_all(flattened[0], ("grp", "sp"), split_axis=0, concat_axis=1, tiled=True),
        lax.all_to_all(flattened[1], ("grp", "sp"), split_axis=0, concat_axis=1, tiled=True),
        lax.all_to_all(flattened[2], ("grp", "sp"), split_axis=0, concat_axis=1, tiled=True),
    )
    frame_local = routed[0].shape[0]
    spatial_len = routed[0].shape[1]
    current_clip = clip_plan[group_index]
    frame_limit = frames_per_clip[current_clip]
    live_count = latent_height[current_clip] * latent_width[current_clip]
    spatial = attend_frames(
        routed[0], routed[1], routed[2], shard_index * frame_local, frame_limit, live_count
    )
    head_count = row_width // HEAD_DIM
    stacked = spatial.reshape(frame_local, spatial_len, head_count, HEAD_DIM)
    per_shard = spatial_len // lax.axis_size("sp")
    first_position = shard_index * per_shard
    arrived = lax.all_to_all(stacked, "sp", split_axis=1, concat_axis=0, tiled=True)
    temporal = temporal_mix(arrived, query_gain, key_gain, frame_limit, live_count, first_position)
    returned = lax.all_to_all(temporal, "sp", split_axis=0, concat_axis=1, tiled=True)
    summed = stacked.astype(jnp.float32) + returned.astype(jnp.float32)
    return summed.astype(jnp.bfloat16).reshape(1, frame_local, spatial_len, row_width)


def solution(mesh):
    in_specs = (
        P(None, None, ("grp", "sp"), None),
        P(None, None, ("grp", "sp"), None),
        P(None, None, ("grp", "sp"), None),
        P(),
        P(),
        P(),
        P(),
        P(),
        P(),
    )
    out_specs = P("grp", "sp", None, None)
    return jax.shard_map(
        on_device, mesh=mesh, in_specs=in_specs, out_specs=out_specs, check_vma=False
    )
```

profile of v0, /device:TPU:0, one launch (start us, length us, event | category | flops | bytes accessed | tf_op | source)
XLA Modules:
  0.0 147.8 jit_solution(17642902807063637534)
XLA Ops:
  0.0 0.0 copy-start
  0.0 0.8 compare_select_fusion
  0.8 0.7 compare_and_fusion
  1.4 0.0 copy-done
  1.5 2.2 %gather_fusion = bf16[8,16,2,1536]{3,2,1,0:T(2,128)(2,1)S(1)} fusion(bf16[16,16,2,1536]{3,2,1,0:T(2,128)(2,1)S(1)} %copy-done, s32[1024]{0:T(1024)S(1)} %pad_clamp_fusion), kind=kCustom, calls=%fused_computation.clone | custom fusion | bytes 1572896 | tf_op jit(solution)/shard_map/jit(_take)/gather | solution.py:79
  3.7 4.4 %gather_fusion.1 = bf16[8,16,2,1536]{3,2,1,0:T(2,128)(2,1)} fusion(bf16[16,16,2,1536]{3,2,1,0:T(2,128)(2,1)} %param.11, s32[1024]{0:T(1024)S(1)} %pad_clamp_fusion), kind=kCustom, calls=%fused_computation.1.clone | custom fusion | bytes 1572896 | tf_op jit(solution)/shard_map/jit(_take)/gather | solution.py:79
  8.0 4.4 %gather_fusion.2 = bf16[8,16,2,1536]{3,2,1,0:T(2,128)(2,1)} fusion(bf16[16,16,2,1536]{3,2,1,0:T(2,128)(2,1)} %param.12, s32[1024]{0:T(1024)S(1)} %pad_clamp_fusion), kind=kCustom, calls=%fused_computation.2.clone | custom fusion | bytes 1572896 | tf_op jit(solution)/shard_map/jit(_take)/gather | solution.py:79
  12.4 4.0 %broadcast_select_fusion.2 = (bf16[8,16,2,1536]{3,2,1,0:T(2,128)(2,1)}, bf16[8,16,2,1536]{3,2,1,0:T(2,128)(2,1)S(1)}, bf16[8,16,2,1536]{3,2,1,0:T(2,128)(2,1)S(1)}) fusion(bf16[8,16,2,1536]{3,2,1,0:T(2,128)(2,1)S(1)} %gather_fusion, pred[8]{0:T(512)(128)(4,1)S(1)} %compare_and_fusion, bf16[8,16,2,1536]{3,2,1,0:T(2,128)(2,1)} %gather_fusion.1, ...), kind=kLoop, calls=%fused_computation.31 | loop fusion | flops 1179648 | bytes 4718600 | tf_op jit(solution)/shard_map/jit(_take)/select_n | solution.py:79
  16.5 27.3 %all_to_all.23 = bf16[128,2,1536]{2,1,0:T(2,128)(2,1)S(1)} all-to-all(bf16[128,2,1536]{2,1,0:T(2,128)(2,1)S(1)} %bitcast.31), channel_id=1, replica_groups=mesh['grp'=8,'sp'=16] {'grp','sp'}, dimensions={0} | all-to-all | bytes 1572864 | tf_op jit(solution)/shard_map/all_to_all | solution.py:85
  43.8 0.0 copy-start.5
  43.8 0.0 copy-start.6
  43.8 0.0 copy-start.7
  43.8 0.0 copy-start.8
  43.8 21.1 %all_to_all.24 = bf16[128,2,1536]{2,1,0:T(2,128)(2,1)} all-to-all(bf16[128,2,1536]{2,1,0:T(2,128)(2,1)S(1)} %bitcast.30), channel_id=1, replica_groups=mesh['grp'=8,'sp'=16] {'grp','sp'}, dimensions={0} | all-to-all | bytes 1572864 | tf_op jit(solution)/shard_map/all_to_all | solution.py:86
  64.9 4.8 %all-to-all-start = ((bf16[128,2,1536]{2,1,0:T(2,128)(2,1)}), bf16[128,2,1536]{2,1,0:T(2,128)(2,1)S(1)}, u32[]{:S(2)}, u32[]{:S(2)}) async-start(bf16[128,2,1536]{2,1,0:T(2,128)(2,1)} %bitcast.3), calls=%async_computation | async-start | bytes 1572864 | tf_op jit(solution)/shard_map/all_to_all | solution.py:87
  69.7 0.0 copy-done.5
  69.7 0.6 dynamic_slice.12
  72.2 0.0 copy-done.6
  72.2 0.6 dynamic_slice.13
  72.8 0.0 copy-done.7
  72.8 0.6 dynamic_slice.14
  73.4 0.0 copy-done.8
  73.4 0.6 dynamic_slice.15
  76.0 1.5 %reshape_squeeze.10 = bf16[256,12,128]{2,1,0:T(8,128)(2,1)} reshape(bf16[128,2,1536]{2,1,0:T(2,128)(2,1)S(1)} %all_to_all.23) | data formatting | bytes 1572864 | tf_op jit(solution)/shard_map/reshape;squeeze | solution.py:21
  77.5 3.2 %reshape_squeeze.11 = bf16[256,12,128]{2,1,0:T(8,128)(2,1)} reshape(bf16[128,2,1536]{2,1,0:T(2,128)(2,1)} %all_to_all.24) | data formatting | bytes 1572864 | tf_op jit(solution)/shard_map/reshape;squeeze | solution.py:18
  80.7 2.2 %fusion = (f32[12,256]{1,0:T(8,128)S(1)}, f32[12,256,256]{1,2,0:T(8,128)S(1)}) fusion(pred[256]{0:T(512)(128)(4,1)S(1)} %get-tuple-element.15, bf16[256,12,128]{2,1,0:T(8,128)(2,1)} %reshape_squeeze.11, bf16[256,12,128]{2,1,0:T(8,128)(2,1)} %reshape_squeeze.10), kind=kOutput, calls=%fused_computation.5 | convolution fusion | flops 203682816 | bytes 4731136 | tf_op jit(solution)/shard_map/qhd,khd->hqk/dot_general | solution.py:23
  83.0 0.0 copy-start.2
  83.0 1.6 %copy-done.2 = f32[12,256,256]{1,2,0:T(8,128)} copy-done((f32[12,256,256]{1,2,0:T(8,128)}, f32[12,256,256]{1,2,0:T(8,128)S(1)}, u32[]{:S(2)}) %copy-start.2) | copy-done | bytes 3145752
  84.6 0.7 fusion.1
  85.4 0.5 all-to-all-done
  85.8 1.5 %reshape_squeeze.9 = bf16[256,12,128]{2,1,0:T(8,128)(2,1)} reshape(bf16[128,2,1536]{2,1,0:T(2,128)(2,1)S(1)} %all-to-all-done) | data formatting | bytes 1572864 | tf_op jit(solution)/shard_map/reshape;squeeze | solution.py:19
  87.4 3.2 %fusion.8 = bf16[256,12,128]{0,2,1:T(8,128)(2,1)S(1)} fusion(f32[12,256,256]{1,2,0:T(8,128)} %copy-done.2, f32[12,256]{1,0:T(8,128)S(1)} %get-tuple-element.11, pred[256]{0:T(512)(128)(4,1)S(1)} %get-tuple-element.15, bf16[256,12,128]{2,1,0:T(8,128)(2,1)} %reshape_squeeze.9, f32[256,12]{0,1:T(8,128)S(1)} %bitcast.36, pred[256]{0:T(512)(128)(4,1)S(1)} %get-tuple-element.16), kind=kOutput, calls=%fused_computation.15 | convolution fusion | flops 205651968 | bytes 4743680 | tf_op jit(solution)/shard_map/hqk,khd->qhd/dot_general | solution.py:31
  90.5 0.0 copy-start.1
  90.5 1.7 %copy.62 = bf16[1,256,12,128]{3,2,0,1:T(8,128)(2,1)} copy(bf16[1,256,12,128]{1,3,2,0:T(8,128)(2,1)S(1)} %bitcast.32) | data formatting | bytes 1572864 | tf_op jit(solution)/shard_map/convert_element_type | solution.py:35
  92.3 0.0 copy-done.1
  92.3 5.6 %all-to-all-start.3 = ((bf16[1,256,12,128]{3,2,0,1:T(8,128)(2,1)}), bf16[1,256,12,128]{3,2,0,1:T(8,128)(2,1)S(1)}, u32[]{:S(2)}, u32[]{:S(2)}) async-start(bf16[1,256,12,128]{3,2,0,1:T(8,128)(2,1)} %copy.62), calls=%async_computation.3 | async-start | bytes 2097152 | tf_op jit(solution)/shard_map/all_to_all | solution.py:101
  97.9 0.7 add_compare_fusion
  98.6 0.1 broadcast_and_fusion
  98.7 0.0 copy-start.3
  98.7 0.0 copy-start.4
  98.7 17.3 %all-to-all-done.3 = bf16[1,256,12,128]{3,2,0,1:T(8,128)(2,1)S(1)} async-done(((bf16[1,256,12,128]{3,2,0,1:T(8,128)(2,1)}), bf16[1,256,12,128]{3,2,0,1:T(8,128)(2,1)S(1)}, u32[]{:S(2)}, u32[]{:S(2)}) %all-to-all-start.3) | async-done | bytes 786464 | tf_op jit(solution)/shard_map/all_to_all | solution.py:101
  116.0 0.6 multiply_reduce_fusion
  116.7 0.1 copy.64
  116.8 0.1 rsqrt.12
  116.9 0.2 copy.63
  117.1 0.0 copy-done.3
  117.1 0.0 copy-done.4
  117.1 0.5 fusion.13
  117.6 3.8 %fusion.35 = (f32[16,12,16]{2,1,0:T(8,128)S(1)}, f32[16,12,16,16]{2,3,1,0:T(8,128)S(1)}) fusion(f32[16,16,12,128]{3,1,0,2:T(8,128)S(1)} %get-tuple-element.7, f32[16,16,12,128]{3,1,0,2:T(8,128)S(1)} %get-tuple-element.6, pred[16]{0:T(512)(128)(4,1)S(1)} %get-tuple-element.18), kind=kOutput, calls=%fused_computation.52 | convolution fusion | flops 75641856 | bytes 3354640 | tf_op jit(solution)/shard_map/fshd,gshd->shfg/dot_general | solution.py:47
  121.4 0.5 fusion.22
  121.9 1.1 fusion.6
  123.1 0.5 copy.69
  123.6 16.3 %all_to_all.50 = bf16[16,16,12,128]{3,1,2,0:T(8,128)(2,1)S(1)} all-to-all(bf16[16,16,12,128]{3,1,2,0:T(8,128)(2,1)S(1)} %copy.69), channel_id=1, replica_groups=mesh['grp'=8,'sp'=16] {'sp'}, dimensions={0} | all-to-all | bytes 1572864 | tf_op jit(solution)/shard_map/all_to_all | solution.py:103
  139.9 0.2 copy.70
  140.1 1.4 bitcast_convert_fusion
  141.4 1.9 %copy.71 = f32[256,12,128]{0,2,1:T(8,128)S(1)} copy(f32[256,12,128]{2,0,1:T(8,128)} %bitcast_convert_fusion) | data formatting | bytes 3145728 | tf_op jit(solution)/shard_map/convert_element_type | solution.py:104
  143.3 2.2 %add_convert_fusion = bf16[256,12,128]{0,2,1:T(8,128)(2,1)} fusion(f32[256,12,128]{0,2,1:T(8,128)S(1)} %copy.71, bf16[256,12,128]{0,2,1:T(8,128)(2,1)} %copy-done.1), kind=kLoop, calls=%fused_computation.19 | loop fusion | flops 1179648 | bytes 3145728 | tf_op jit(solution)/shard_map/convert_element_type | solution.py:105
  145.5 2.3 %copy.72 = bf16[1,1,256,1536]{3,2,1,0:T(8,128)(2,1)} copy(bf16[1,1,256,1536]{2,3,1,0:T(8,128)(2,1)} %bitcast.34) | data formatting | bytes 1572864 | tf_op jit(solution)/shard_map/reshape | solution.py:105
  (3 shorter events, 0.0 us)
Async XLA Ops:
  0.0 1.5 copy-start
  43.8 26.0 %copy-start.5 = (s32[8]{0:T(128)S(1)}, s32[8]{0:T(128)}, u32[]{:S(2)}) copy-start(s32[8]{0:T(128)} %param.19) | copy-start | bytes 100
  43.8 28.4 %copy-start.6 = (s32[16]{0:T(128)S(1)}, s32[16]{0:T(128)}, u32[]{:S(2)}) copy-start(s32[16]{0:T(128)} %param.17) | copy-start | bytes 196
  43.8 29.0 %copy-start.7 = (s32[16]{0:T(128)S(1)}, s32[16]{0:T(128)}, u32[]{:S(2)}) copy-start(s32[16]{0:T(128)} %param.18) | copy-start | bytes 196
  43.8 29.7 %copy-start.8 = (s32[16]{0:T(128)S(1)}, s32[16]{0:T(128)}, u32[]{:S(2)}) copy-start(s32[16]{0:T(128)} %param.16) | copy-start | bytes 196
  64.9 21.0 %all-to-all-start = ((bf16[128,2,1536]{2,1,0:T(2,128)(2,1)}), bf16[128,2,1536]{2,1,0:T(2,128)(2,1)S(1)}, u32[]{:S(2)}, u32[]{:S(2)}) async-start(bf16[128,2,1536]{2,1,0:T(2,128)(2,1)} %bitcast.3), calls=%async_computation | async-start | bytes 1572864 | tf_op jit(solution)/shard_map/all_to_all | solution.py:87
  83.0 1.6 %copy-start.2 = (f32[12,256,256]{1,2,0:T(8,128)}, f32[12,256,256]{1,2,0:T(8,128)S(1)}, u32[]{:S(2)}) copy-start(f32[12,256,256]{1,2,0:T(8,128)S(1)} %get-tuple-element.12) | copy-start | bytes 9437188
  90.5 1.8 %copy-start.1 = (bf16[256,12,128]{0,2,1:T(8,128)(2,1)}, bf16[256,12,128]{0,2,1:T(8,128)(2,1)S(1)}, u32[]{:S(2)}) copy-start(bf16[256,12,128]{0,2,1:T(8,128)(2,1)S(1)} %fusion.8) | copy-start | bytes 2359300
  92.3 23.8 %all-to-all-start.3 = ((bf16[1,256,12,128]{3,2,0,1:T(8,128)(2,1)}), bf16[1,256,12,128]{3,2,0,1:T(8,128)(2,1)S(1)}, u32[]{:S(2)}, u32[]{:S(2)}) async-start(bf16[1,256,12,128]{3,2,0,1:T(8,128)(2,1)} %copy.62), calls=%async_computation.3 | async-start | bytes 2097152 | tf_op jit(solution)/shard_map/all_to_all | solution.py:101
  98.7 18.4 %copy-start.3 = (f32[128]{0:T(128)S(1)}, f32[128]{0:T(128)}, u32[]{:S(2)}) copy-start(f32[128]{0:T(128)} %param.14) | copy-start | bytes 1540
  98.7 18.4 %copy-start.4 = (f32[128]{0:T(128)S(1)}, f32[128]{0:T(128)}, u32[]{:S(2)}) copy-start(f32[128]{0:T(128)} %param.15) | copy-start | bytes 1540
where the time goes:
time: 148 us
  blocking collectives  64.7 us (44%)
  local copies, waits for them, and re-layouts  28.3 us (19%)
  waiting for transfers between devices  17.8 us (12%)
  other arithmetic  12.3 us (8%)
  starting transfers between devices  10.4 us (7%)
  matrix products  10.3 us (7%)
  between operations  4.01 us (3%)
    all_to_all x1, blocking collectives, on_device(): lax.all_to_all(flattened[0], ('grp', 'sp'), split_axis=0, concat_axis=1,...  27.3 us
    all_to_all x1, blocking collectives, on_device(): lax.all_to_all(flattened[1], ('grp', 'sp'), split_axis=0, concat_axis=1,...  21.1 us
    all_to_all x1, waiting for transfers between devices, on_device(): lax.all_to_all(stacked, 'sp', split_axis=1, concat_axis=0, tiled=True)  17.3 us
    all_to_all x1, blocking collectives, on_device(): lax.all_to_all(temporal, 'sp', split_axis=0, concat_axis=1, tiled=True)  16.3 us
    gather x3, local copies, waits for them, and re-layouts, on_device(): jnp.take(tensor, clip_plan, axis=0)  11 us
    all_to_all x1, starting transfers between devices, on_device(): lax.all_to_all(stacked, 'sp', split_axis=1, concat_axis=0, tiled=True)  5.64 us
    select_n x2, other arithmetic, on_device(): jnp.take(tensor, clip_plan, axis=0)  4.82 us
    all_to_all x1, starting transfers between devices, on_device(): lax.all_to_all(flattened[2], ('grp', 'sp'), split_axis=0, concat_axis=1,...  4.81 us
  transfers between devices with their start and end apart: 2, of which 2 were waited for; matrix products, arithmetic and copies ran while one was open for 7% of the time, Pallas kernels for 0%

commit v1 on v0

v1 whole, which is shorter than its diff:
```python
import functools
import math

import jax
import jax.numpy as jnp
from jax import lax
from jax.experimental import pallas as pl
from jax.experimental.pallas import tpu as pltpu
from jax.sharding import PartitionSpec as P

MESH = pl.DeviceIdType.MESH
D = 128
HEADS = 12
FRAMES = 16
POS = 256
DEVS = 128
CHUNKS = 2
FC = FRAMES // CHUNKS
PCHUNKS = 4
PC = POS // PCHUNKS
LOG2E = math.log2(math.e)
SCALE = D**-0.5


def idle_rank(z, c, x, y):
    return lax.rem(x + y + z - 2 * c + 8, 4)


def kernel(
    plan, frames, height, width, q_hbm, k_hbm, v_hbm, gq, gk, out,
    xq, xk, xv, stage, recv, spat, sendbuf,
    x_sem, in_send, in_recv, out_send, out_recv, ready,
):
    my_g = lax.axis_index("grp")
    my_s = lax.axis_index("sp")
    me = my_g * 16 + my_s
    mz, mc = lax.div(my_g, 2), lax.rem(my_g, 2)
    mx, my = lax.div(my_s, 4), lax.rem(my_s, 4)
    my_rank = idle_rank(mz, mc, mx, my)
    active = my_rank > 0
    my_head = jnp.maximum(mx * 3 + my_rank - 1, 0)

    barrier = pltpu.get_barrier_semaphore()

    def greet_grp(i, _):
        pl.semaphore_signal(barrier, 1, device_id=(lax.rem(my_g + i, 8), my_s), device_id_type=MESH)
        return 0

    def greet_sp(i, _):
        pl.semaphore_signal(barrier, 1, device_id=(my_g, lax.rem(my_s + i, 16)), device_id_type=MESH)
        return 0

    def greet_all(i, _):
        pl.semaphore_signal(ready, 1, device_id=(my_g, lax.rem(my_s + i, 16)), device_id_type=MESH)
        return 0

    lax.fori_loop(1, 8, greet_grp, 0)
    lax.fori_loop(1, 16, greet_sp, 0)
    loads = [
        pltpu.make_async_copy(ref, held, x_sem.at[t])
        for t, (ref, held) in enumerate(((q_hbm, xq), (k_hbm, xk), (v_hbm, xv)))
    ]
    for copy in loads:
        copy.start()
    pl.semaphore_wait(barrier, 22)
    lax.fori_loop(1, 16, greet_all, 0)

    stage_rows = stage.reshape(8, 3, FRAMES * HEADS * 2, D)
    for t, held in enumerate((xq, xk, xv)):
        loads[t].wait()
        x_rows = held.reshape(16, FRAMES * HEADS * 2, D)

        def pick(g, _):
            stage_rows[g, t] = x_rows[plan[g]]
            return 0

        lax.fori_loop(0, 8, pick, 0)
    pl.semaphore_wait(ready, 15)

    for ch in range(CHUNKS):
        span = pl.ds(ch * FC, FC)

        def send_unit(i, _):
            j = lax.rem(i * 45, 128)
            c = lax.rem(mc + lax.rem(j, 2), 2)
            z = lax.rem(mz + lax.rem(lax.div(j, 2), 4), 4)
            x = lax.rem(mx + lax.rem(lax.div(j, 8), 4), 4)
            y = lax.rem(my + lax.div(j, 32), 4)
            rank = idle_rank(z, c, x, y)
            g, s = z * 2 + c, x * 4 + y
            head = jnp.maximum(x * 3 + rank - 1, 0)
            src = stage.at[g, :, span, head]
            dst = recv.at[:, span, me]

            @pl.when((rank > 0) & (j != 0))
            def _():
                pltpu.make_async_remote_copy(
                    src, dst, in_send, in_recv.at[ch], device_id=(g, s), device_id_type=MESH
                ).start()

            @pl.when((rank > 0) & (j == 0))
            def _():
                pltpu.make_async_copy(src, dst, in_recv.at[ch]).start()

            return 0

        lax.fori_loop(0, 128, send_unit, 0)

    @pl.when(active)
    def _():
        clip = plan[my_g]
        live_frames = frames[clip]
        live_pos = height[clip] * width[clip]
        rows = recv.reshape(3, FRAMES, POS, D)
        key_ids = lax.broadcasted_iota(jnp.int32, (1, POS), 1)
        key_bias = jnp.where(key_ids < live_pos, 0.0, -jnp.inf).astype(jnp.float32)
        row_ids = lax.broadcasted_iota(jnp.int32, (POS, 1), 0)
        row_live = jnp.where(row_ids < live_pos, 1.0, 0.0).astype(jnp.float32)

        def spatial(f, _):
            scores = lax.dot_general(
                rows[0, f], rows[1, f], (((1,), (1,)), ((), ())), preferred_element_type=jnp.float32
            )
            scores = scores + key_bias
            top = jnp.max(scores, axis=-1, keepdims=True)
            weights = jnp.exp2((scores - top) * (SCALE * LOG2E))
            total = jnp.sum(weights, axis=-1, keepdims=True)
            mixed = jnp.dot(weights.astype(jnp.bfloat16), rows[2, f], preferred_element_type=jnp.float32)
            on = jnp.where(f < live_frames, 1.0, 0.0).astype(jnp.float32)
            mixed = (mixed / total) * (row_live * on)
            spat[f] = mixed.astype(jnp.bfloat16).astype(jnp.float32)
            return 0

        for ch in range(CHUNKS):
            part = recv.at[:, pl.ds(ch * FC, FC)]
            pltpu.make_async_copy(part, part, in_recv.at[ch]).wait()
            lax.fori_loop(ch * FC, (ch + 1) * FC, spatial, 0)

        gain = (gq[...] * gk[...]) * (SCALE * LOG2E)
        B = 8
        T = FRAMES * B
        r_id = lax.broadcasted_iota(jnp.int32, (T, T), 0)
        c_id = lax.broadcasted_iota(jnp.int32, (T, T), 1)
        pair_on = (lax.rem(r_id, B) == lax.rem(c_id, B)) & (lax.div(c_id, B) < live_frames)
        pair_bias = jnp.where(pair_on, 0.0, -jnp.inf).astype(jnp.float32)
        t_id = lax.broadcasted_iota(jnp.int32, (T, 1), 0)
        t_pos = lax.rem(t_id, B)
        t_on = lax.div(t_id, B) < live_frames

        def temporal(p0):
            x = spat[:, pl.ds(p0, B), :].reshape(T, D)
            inv = lax.rsqrt(jnp.sum(x * x, axis=-1, keepdims=True) * (1.0 / D) + 1e-6)
            xb = x.astype(jnp.bfloat16)
            y = x * inv * gain
            hi = y.astype(jnp.bfloat16)
            lo = (y - hi.astype(jnp.float32)).astype(jnp.bfloat16)
            scores = lax.dot_general(
                jnp.concatenate([xb, xb], axis=1), jnp.concatenate([hi, lo], axis=1),
                (((1,), (1,)), ((), ())), preferred_element_type=jnp.float32,
            )
            scores = scores * inv + pair_bias
            top = jnp.max(scores, axis=-1, keepdims=True)
            weights = jnp.exp2(scores - top)
            total = jnp.sum(weights, axis=-1, keepdims=True)
            mixed = jnp.dot(weights.astype(jnp.bfloat16), xb, preferred_element_type=jnp.float32)
            live = jnp.where(t_on & (t_pos + p0 < live_pos), 1.0, 0.0).astype(jnp.float32)
            mixed = ((mixed / total) * live).astype(jnp.bfloat16).astype(jnp.float32)
            return (x + mixed).reshape(FRAMES, B, D)

        column = pl.ds(pl.multiple_of(my_head * D, D), D)
        for pc in range(PCHUNKS):

            def blocks(b, _):
                p0 = pl.multiple_of(pc * PC + b * 16, 16)
                pair = jnp.concatenate([temporal(p0), temporal(p0 + 8)], axis=1)
                sendbuf[:, pl.ds(p0, 16), :] = pair.astype(jnp.bfloat16)
                return 0

            lax.fori_loop(0, PC // 16, blocks, 0)
            span = pl.ds(pc * PC, PC)

            def send_frame(i, _):
                f = lax.rem(my_s + i, 16)
                pltpu.make_async_remote_copy(
                    sendbuf.at[f, span], out.at[0, 0, span, column], out_send, out_recv,
                    device_id=(my_g, f), device_id_type=MESH,
                ).start()
                return 0

            lax.fori_loop(1, 16, send_frame, 0)
            pltpu.make_async_copy(sendbuf.at[my_s, span], out.at[0, 0, span, column], out_recv).start()

        sent = recv.at[:, :, pl.ds(0, 95)]
        pltpu.make_async_copy(sent, sent, in_send).wait()
        mine = sendbuf.at[pl.ds(0, 15)]
        pltpu.make_async_copy(mine, mine, out_send).wait()

    @pl.when(jnp.logical_not(active))
    def _():
        sent = recv.at[:, :, pl.ds(0, 96)]
        pltpu.make_async_copy(sent, sent, in_send).wait()

    pltpu.make_async_copy(out, out, out_recv).wait()


def on_device(
    queries, key_rows, values, query_gain, key_gain, frames_per_clip, latent_height, latent_width, clip_plan
):
    def by_head(x):
        return x.reshape(16, FRAMES, 2, HEADS, D).transpose(0, 1, 3, 2, 4)

    smem = pl.BlockSpec(memory_space=pltpu.SMEM)
    hbm = pl.BlockSpec(memory_space=pl.ANY)
    vmem = pl.BlockSpec(memory_space=pltpu.VMEM)
    return pl.pallas_call(
        kernel,
        out_shape=jax.ShapeDtypeStruct((1, 1, POS, HEADS * D), jnp.bfloat16),
        in_specs=[smem] * 4 + [hbm] * 3 + [vmem] * 2,
        out_specs=hbm,
        scratch_shapes=[
            pltpu.VMEM((16, FRAMES, HEADS, 2, D), jnp.bfloat16),
            pltpu.VMEM((16, FRAMES, HEADS, 2, D), jnp.bfloat16),
            pltpu.VMEM((16, FRAMES, HEADS, 2, D), jnp.bfloat16),
            pltpu.VMEM((8, 3, FRAMES, HEADS, 2, D), jnp.bfloat16),
            pltpu.VMEM((3, FRAMES, DEVS, 2, D), jnp.bfloat16),
            pltpu.VMEM((FRAMES, POS, D), jnp.float32),
            pltpu.VMEM((FRAMES, POS, D), jnp.bfloat16),
            pltpu.SemaphoreType.DMA((3,)),
            pltpu.SemaphoreType.DMA,
            pltpu.SemaphoreType.DMA((CHUNKS,)),
            pltpu.SemaphoreType.DMA,
            pltpu.SemaphoreType.DMA,
            pltpu.SemaphoreType.REGULAR,
        ],
        compiler_params=pltpu.CompilerParams(
            collective_id=0, has_side_effects=True, vmem_limit_bytes=48 << 20
        ),
        name="attend",
    )(
        clip_plan, frames_per_clip, latent_height, latent_width,
        by_head(queries), by_head(key_rows), by_head(values),
        query_gain.reshape(1, D), key_gain.reshape(1, D),
    )


def solution(mesh):
    split = P(None, None, ("grp", "sp"), None)
    return jax.shard_map(
        on_device,
        mesh=mesh,
        in_specs=(split, split, split, P(), P(), P(), P(), P(), P()),
        out_specs=P("grp", "sp", None, None),
        check_vma=False,
    )
```

time: 148 us -> 81.6 us (0.55)
  Pallas kernels: 0 us -> 72.3 us
  blocking collectives: 64.7 us -> 0 us
  local copies, waits for them, and re-layouts: 28.3 us -> 9.03 us
  waiting for transfers between devices: 17.8 us -> 0 us
  other arithmetic: 12.3 us -> 0 us
  starting transfers between devices: 10.4 us -> 0 us
  matrix products: 10.3 us -> 0 us
  between operations: 4.01 us -> 0.02 us
    pallas_call x0 -> x1, Pallas kernels: none -> 72.3 us  [on_device(): pl.pallas_call(kernel, out_shape=jax.ShapeDtypeStruct((1, 1, POS, HEADS *...]
    all_to_all x3 -> x0, blocking collectives: 64.7 us -> none  [the longest x1 27.3 us: on_device(): lax.all_to_all(flattened[0], ('grp', 'sp'), split_axis=0, concat_axis=1,...]
    all_to_all x2 -> x0, waiting for transfers between devices: 17.8 us -> none  [the longest x1 17.3 us: on_device(): lax.all_to_all(stacked, 'sp', split_axis=1, concat_axis=0, tiled=True)]
    gather x3 -> x0, local copies, waits for them, and re-layouts: 11 us -> none  [on_device(): jnp.take(tensor, clip_plan, axis=0)]
    all_to_all x2 -> x0, starting transfers between devices: 10.4 us -> none  [the longest x1 5.64 us: on_device(): lax.all_to_all(stacked, 'sp', split_axis=1, concat_axis=0, tiled=True)]
    dot_general x4 -> x0, matrix products: 10.3 us -> none  [the longest x1 3.78 us: temporal_mix(): jnp.einsum('fshd,gshd->shfg', query_side, key_side, precision=lax.Precisi...]
    unnamed x18 -> x19, local copies, waits for them, and re-layouts: 1.67 us -> 9.03 us
    another operation x3 -> x0, local copies, waits for them, and re-layouts: 6.25 us -> none  [the longest x1 3.21 us: attend_frames(): key_heads = routed_keys[0].reshape(spatial_len, head_count, HEAD_DIM)]
  transfers between devices with their start and end apart: 2 -> 0, of which waited for: 2 -> 0; matrix products, arithmetic and copies ran while one was open for 7% -> 0% of each run, Pallas kernels for 0% -> 0%
where the time goes in v1:
time: 81.6 us; the launch traced here: 81.4 us
  Pallas kernels  72.3 us (89%)
  local copies, waits for them, and re-layouts  9.03 us (11%)
    pallas_call x1, Pallas kernels, on_device(): pl.pallas_call(kernel, out_shape=jax.ShapeDtypeStruct((1, 1, POS, HEADS *...  72.3 us
    unnamed x19, local copies, waits for them, and re-layouts  9.03 us

profile of v1, /device:TPU:0, one launch (start us, length us, event | category | flops | bytes accessed | tf_op | source)
XLA Modules:
  0.0 81.4 jit_solution(8749515292613409264)
XLA Ops:
  0.0 0.0 copy-start
  0.0 1.4 %copy-done = bf16[16,16,2,1536]{3,2,1,0:T(2,128)(2,1)S(1)} copy-done((bf16[16,16,2,1536]{3,2,1,0:T(2,128)(2,1)S(1)}, bf16[16,16,2,1536]{3,2,1,0:T(2,128)(2,1)}, u32[]{:S(2)}) %copy-start) | copy-done | bytes 1572888
  1.4 0.0 copy-start.1
  1.4 1.4 %copy-done.1 = bf16[16,16,2,1536]{3,2,1,0:T(2,128)(2,1)S(1)} copy-done((bf16[16,16,2,1536]{3,2,1,0:T(2,128)(2,1)S(1)}, bf16[16,16,2,1536]{3,2,1,0:T(2,128)(2,1)}, u32[]{:S(2)}) %copy-start.1) | copy-done | bytes 1572888
  2.8 0.0 copy-start.2
  2.8 1.4 %copy-done.2 = bf16[16,16,2,1536]{3,2,1,0:T(2,128)(2,1)S(1)} copy-done((bf16[16,16,2,1536]{3,2,1,0:T(2,128)(2,1)S(1)}, bf16[16,16,2,1536]{3,2,1,0:T(2,128)(2,1)}, u32[]{:S(2)}) %copy-start.2) | copy-done | bytes 1572888
  4.2 0.0 copy-start.3
  4.2 0.7 copy-done.3
  4.9 0.0 copy-start.4
  4.9 0.7 copy-done.4
  5.5 0.0 copy-start.5
  5.5 0.7 copy-done.5
  6.2 0.0 copy-start.6
  6.2 0.7 copy-done.6
  6.8 0.0 copy-start.7
  6.9 0.7 copy-done.7
  7.5 0.0 copy-start.8
  7.5 0.7 copy-done.8
  8.2 72.3 %attend.1 = bf16[1,1,256,1536]{3,2,1,0:T(8,128)(2,1)S(1)} custom-call(s32[8]{0:T(128)S(1)} %copy-done.3, s32[16]{0:T(128)S(1)} %copy-done.4, s32[16]{0:T(128)S(1)} %copy-done.5, s32[16]{0:T(128)S(1)} %copy-done.6, bf16[16,16,12,2,128]{4,3,2,1,0:T(2,128)(2,1)S(1)} %bitcast.11, bf16[16,16,12,2,128]{4,3,2,1,0:T(2,128)(2,1)S(1)} %bitcast.12, ...), custom_call_target="tpu_custom_call" | custom-call | tf_op jit(solution)/shard_map/attend/pallas_call | solution.py:215
  80.5 0.9 %copy.11 = bf16[1,1,256,1536]{3,2,1,0:T(8,128)(2,1)} copy(bf16[1,1,256,1536]{3,2,1,0:T(8,128)(2,1)S(1)} %attend.1) | data formatting | bytes 1572864
Async XLA Ops:
  0.0 1.4 %copy-start = (bf16[16,16,2,1536]{3,2,1,0:T(2,128)(2,1)S(1)}, bf16[16,16,2,1536]{3,2,1,0:T(2,128)(2,1)}, u32[]{:S(2)}) copy-start(bf16[16,16,2,1536]{3,2,1,0:T(2,128)(2,1)} %param.9) | copy-start | bytes 4718596
  1.4 1.4 %copy-start.1 = (bf16[16,16,2,1536]{3,2,1,0:T(2,128)(2,1)S(1)}, bf16[16,16,2,1536]{3,2,1,0:T(2,128)(2,1)}, u32[]{:S(2)}) copy-start(bf16[16,16,2,1536]{3,2,1,0:T(2,128)(2,1)} %param.10) | copy-start | bytes 4718596
  2.8 1.4 %copy-start.2 = (bf16[16,16,2,1536]{3,2,1,0:T(2,128)(2,1)S(1)}, bf16[16,16,2,1536]{3,2,1,0:T(2,128)(2,1)}, u32[]{:S(2)}) copy-start(bf16[16,16,2,1536]{3,2,1,0:T(2,128)(2,1)} %param.11) | copy-start | bytes 4718596
  4.2 0.7 copy-start.3
  4.9 0.7 copy-start.4
  5.5 0.7 copy-start.5
  6.2 0.7 copy-start.6
  6.8 0.7 copy-start.7
  7.5 0.7 copy-start.8

commit v2 on v1

v2 whole, which is shorter than its diff:
```python
import functools
import math

import jax
import jax.numpy as jnp
from jax import lax
from jax.experimental import pallas as pl
from jax.experimental.pallas import tpu as pltpu
from jax.sharding import PartitionSpec as P

MESH = pl.DeviceIdType.MESH
D = 128
HEADS = 12
FRAMES = 16
POS = 256
DEVS = 128
HALF = FRAMES // 2
BLOCK = 16
PC = 64
VMEM_BYTES = 64 << 20
SU = 4
SCALE2 = D**-0.5 * math.log2(math.e)


def unit_of(z, c, x, y):
    whole = x * 4 + y
    over = jnp.where(whole >= HEADS, 1, 0)
    group = jnp.where(c == 0, 2 * z + over, 2 * z + 1)
    head = jnp.where(c == 0, whole - HEADS * over, 4 + 2 * x + lax.div(y, 2))
    first_frame = jnp.where(c == 0, 0, HALF * lax.rem(y, 2))
    return group, head, first_frame


def kernel(
    plan_hbm, frames_hbm, height_hbm, width_hbm, q_hbm, k_hbm, v_hbm, gq_hbm, gk_hbm, out,
    plan, frames, height, width, gq, gk, xq, xk, xv, stage, recv, spat, sendbuf,
    x_sem, in_send, in_recv, pair_send, pair_recv, out_send, out_recv, ready,
):
    my_g = lax.axis_index("grp")
    my_s = lax.axis_index("sp")
    me = my_g * 16 + my_s
    mz, mc = lax.div(my_g, 2), lax.rem(my_g, 2)
    mx, my = lax.div(my_s, 4), lax.rem(my_s, 4)
    my_unit, my_head, my_first = unit_of(mz, mc, mx, my)

    barrier = pltpu.get_barrier_semaphore()

    def greet_grp(i, _):
        pl.semaphore_signal(barrier, 1, device_id=(lax.rem(my_g + i, 8), my_s), device_id_type=MESH)
        return 0

    def greet_sp(i, _):
        pl.semaphore_signal(barrier, 1, device_id=(my_g, lax.rem(my_s + i, 16)), device_id_type=MESH)
        return 0

    def greet_all(i, _):
        pl.semaphore_signal(ready, 1, device_id=(my_g, lax.rem(my_s + i, 16)), device_id_type=MESH)
        return 0

    lax.fori_loop(1, 8, greet_grp, 0)
    lax.fori_loop(1, 16, greet_sp, 0)
    loads = [
        pltpu.make_async_copy(ref, held, x_sem.at[t])
        for t, (ref, held) in enumerate((
            (plan_hbm, plan), (q_hbm, xq), (k_hbm, xk), (v_hbm, xv), (frames_hbm, frames),
            (height_hbm, height), (width_hbm, width), (gq_hbm, gq), (gk_hbm, gk),
        ))
    ]
    for copy in loads:
        copy.start()
    pl.semaphore_wait(barrier, 22)
    lax.fori_loop(1, 16, greet_all, 0)

    loads[0].wait()
    stage_rows = stage.reshape(8, 3, FRAMES * HEADS * 2, D)
    for t, held in enumerate((xq, xk, xv)):
        loads[1 + t].wait()
        x_rows = held.reshape(16, FRAMES * HEADS * 2, D)

        def pick(g, _):
            stage_rows[g, t] = x_rows[plan[g]]
            return 0

        lax.fori_loop(0, 8, pick, 0)
    for copy in loads[4:]:
        copy.wait()
    pl.semaphore_wait(ready, 15)

    def target(j, c):
        z = lax.rem(mz + lax.rem(j, 4), 4)
        x = lax.rem(mx + lax.rem(lax.div(j, 4), 4), 4)
        y = lax.rem(my + lax.div(j, 16), 4)
        return z, x, y

    def send_unit(part, j, c):
        z, x, y = target(j, c)
        group, head, first = unit_of(z, c, x, y)
        g, s = 2 * z + c, 4 * x + y
        src = stage.at[group, :, pl.ds(first + part * HALF, HALF), head]
        dst = recv.at[:, pl.ds(part * HALF, HALF), me]
        here = (j == 0) & (c == mc)

        @pl.when(jnp.logical_not(here))
        def _():
            pltpu.make_async_remote_copy(
                src, dst, in_send.at[part], in_recv.at[part], device_id=(g, s), device_id_type=MESH
            ).start()

        @pl.when(here)
        def _():
            pltpu.make_async_copy(src, dst, in_recv.at[part]).start()

    def send_first(i, _):
        j = lax.rem(i * 45, 128)
        send_unit(0, lax.div(j, 2), lax.rem(mc + lax.rem(j, 2), 2))
        return 0

    def send_second(i, _):
        send_unit(1, lax.rem(i * 29, 64), 0)
        return 0

    lax.fori_loop(0, 128, send_first, 0)
    lax.fori_loop(0, 64, send_second, 0)

    clip = plan[my_unit]
    live_frames = frames[clip]
    live_pos = height[clip] * width[clip]
    rows = recv.reshape(3, FRAMES, POS, D)
    key_bias = jnp.where(lax.broadcasted_iota(jnp.int32, (1, POS), 1) < live_pos, 0.0, -jnp.inf)
    row_live = jnp.where(lax.broadcasted_iota(jnp.int32, (POS, 1), 0) < live_pos, 1.0, 0.0)
    ones = jnp.ones((POS, D), jnp.bfloat16)

    def spatial(i):
        scores = lax.dot_general(
            rows[0, i], rows[1, i], (((1,), (1,)), ((), ())), preferred_element_type=jnp.float32
        )
        scores = scores + key_bias
        top = jnp.max(scores, axis=-1, keepdims=True)
        weights = jnp.exp2((scores - top) * SCALE2)
        total = jnp.sum(weights, axis=-1, keepdims=True)
        mixed = jnp.dot(weights.astype(jnp.bfloat16), rows[2, i], preferred_element_type=jnp.float32)
        f = my_first + i
        on = jnp.where(f < live_frames, 1.0, 0.0)
        spat[f] = (mixed * (row_live * on / total)).astype(jnp.bfloat16)

    def spatial_part(part):
        arrived = recv.at[:, pl.ds(part * HALF, HALF)]
        pltpu.make_async_copy(arrived, arrived, in_recv.at[part]).wait()

        def four(b, _):
            for k in range(SU):
                spatial(part * HALF + b * SU + k)
            return 0

        lax.fori_loop(0, HALF // SU, four, 0)

    spatial_part(0)

    @pl.when(mc == 0)
    def _():
        spatial_part(1)

    half = lax.rem(my, 2)
    own = pl.ds(pl.multiple_of(half * (POS // 2), POS // 2), POS // 2)
    theirs = pl.ds(pl.multiple_of((1 - half) * (POS // 2), POS // 2), POS // 2)

    @pl.when(mc == 1)
    def _():
        partner = my_s + 1 - 2 * half
        block = spat.at[pl.ds(my_first, HALF), theirs]
        copy = pltpu.make_async_remote_copy(
            block, block, pair_send, pair_recv, device_id=(my_g, partner), device_id_type=MESH
        )
        copy.start()
        copy.wait()

    gain = (gq[...] * gk[...]) * SCALE2
    T = FRAMES * BLOCK
    r_id = lax.broadcasted_iota(jnp.int32, (T, T), 0)
    c_id = lax.broadcasted_iota(jnp.int32, (T, T), 1)
    pair_on = (lax.rem(r_id, BLOCK) == lax.rem(c_id, BLOCK)) & (lax.div(c_id, BLOCK) < live_frames)
    pair_bias = jnp.where(pair_on, 0.0, -jnp.inf)
    t_on = lax.div(lax.broadcasted_iota(jnp.int32, (T, 1), 0), BLOCK) < live_frames
    frame_on = jnp.where(t_on, 1.0, 0.0)

    def temporal(p0):
        xb = spat[:, pl.ds(p0, BLOCK), :].reshape(T, D)
        x = xb.astype(jnp.float32)
        inv = lax.rsqrt(jnp.sum(x * x, axis=-1, keepdims=True) * (1.0 / D) + 1e-6)
        y = x * inv * gain
        hi = y.astype(jnp.bfloat16)
        lo = (y - hi.astype(jnp.float32)).astype(jnp.bfloat16)
        scores = lax.dot_general(
            jnp.concatenate([xb, xb], axis=1), jnp.concatenate([hi, lo], axis=1),
            (((1,), (1,)), ((), ())), preferred_element_type=jnp.float32,
        )
        scores = scores + pair_bias
        top = jnp.max(scores, axis=-1, keepdims=True)
        weights = jnp.exp2((scores - top) * inv)
        total = jnp.sum(weights, axis=-1, keepdims=True)
        mixed = jnp.dot(weights.astype(jnp.bfloat16), xb, preferred_element_type=jnp.float32)
        mixed = (mixed * (frame_on / total)).astype(jnp.bfloat16).astype(jnp.float32)
        sendbuf[:, pl.ds(p0, BLOCK), :] = (x + mixed).astype(jnp.bfloat16).reshape(FRAMES, BLOCK, D)

    column = pl.ds(pl.multiple_of(my_head * D, D), D)
    own_unit = my_unit == my_g

    def chunk(b, _):
        p0 = pl.multiple_of(b * PC, PC)
        for k in range(PC // BLOCK):
            temporal(p0 + k * BLOCK)
        span = pl.ds(p0, PC)

        def send_frame(i, _):
            f = lax.rem(my_s + i, 16)
            src, dst = sendbuf.at[f, span], out.at[0, 0, span, column]
            here = (i == 0) & own_unit

            @pl.when(jnp.logical_not(here))
            def _():
                pltpu.make_async_remote_copy(
                    src, dst, out_send, out_recv, device_id=(my_unit, f), device_id_type=MESH
                ).start()

            @pl.when(here)
            def _():
                pltpu.make_async_copy(src, dst, out_recv).start()

            return 0

        lax.fori_loop(0, 16, send_frame, 0)
        return 0

    first_chunk = jnp.where(mc == 0, 0, half * (POS // 2 // PC))
    last_chunk = jnp.where(mc == 0, POS // PC, first_chunk + POS // 2 // PC)
    lax.fori_loop(first_chunk, last_chunk, chunk, 0)

    def sent(ref, sem):
        pltpu.make_async_copy(ref, ref, sem).wait()

    sent(recv.at[:, pl.ds(0, HALF), pl.ds(0, DEVS - 1)], in_send.at[0])

    @pl.when(mc == 0)
    def _():
        sent(recv.at[:, pl.ds(0, HALF), pl.ds(0, DEVS // 2 - 1)], in_send.at[1])

        @pl.when(own_unit)
        def _():
            sent(sendbuf.at[pl.ds(0, 15)], out_send)

        @pl.when(jnp.logical_not(own_unit))
        def _():
            sent(sendbuf, out_send)

    @pl.when(mc == 1)
    def _():
        sent(recv.at[:, pl.ds(0, HALF), pl.ds(0, DEVS // 2)], in_send.at[1])
        sent(sendbuf.at[pl.ds(0, 15), pl.ds(0, POS // 2)], out_send)

    pltpu.make_async_copy(out, out, out_recv).wait()


def on_device(
    queries, key_rows, values, query_gain, key_gain, frames_per_clip, latent_height, latent_width, clip_plan
):
    def by_head(x):
        return x.reshape(16, FRAMES, 2, HEADS, D).transpose(0, 1, 3, 2, 4)

    hbm = pl.BlockSpec(memory_space=pl.ANY)
    clips = pltpu.VMEM((16, FRAMES, HEADS, 2, D), jnp.bfloat16)
    counts = pltpu.SMEM((16,), jnp.int32)
    dma = pltpu.SemaphoreType.DMA
    return pl.pallas_call(
        kernel,
        out_shape=jax.ShapeDtypeStruct((1, 1, POS, HEADS * D), jnp.bfloat16),
        in_specs=[hbm] * 9,
        out_specs=hbm,
        scratch_shapes=[
            pltpu.SMEM((8,), jnp.int32), counts, counts, counts,
            pltpu.VMEM((1, D), jnp.float32), pltpu.VMEM((1, D), jnp.float32),
            clips, clips, clips,
            pltpu.VMEM((8, 3, FRAMES, HEADS, 2, D), jnp.bfloat16),
            pltpu.VMEM((3, FRAMES, DEVS, 2, D), jnp.bfloat16),
            pltpu.VMEM((FRAMES, POS, D), jnp.bfloat16),
            pltpu.VMEM((FRAMES, POS, D), jnp.bfloat16),
            dma((9,)), dma((2,)), dma((2,)), dma, dma, dma, dma,
            pltpu.SemaphoreType.REGULAR,
        ],
        compiler_params=pltpu.CompilerParams(
            collective_id=0, has_side_effects=True, vmem_limit_bytes=VMEM_BYTES
        ),
        name="attend",
    )(
        clip_plan, frames_per_clip, latent_height, latent_width,
        by_head(queries), by_head(key_rows), by_head(values),
        query_gain.reshape(1, D), key_gain.reshape(1, D),
    )


def solution(mesh):
    split = P(None, None, ("grp", "sp"), None)
    return jax.shard_map(
        on_device,
        mesh=mesh,
        in_specs=(split, split, split, P(), P(), P(), P(), P(), P()),
        out_specs=P("grp", "sp", None, None),
        check_vma=False,
    )
```

time: 81.6 us -> 57.2 us (0.70)
  Pallas kernels: 72.3 us -> 54.8 us
  local copies, waits for them, and re-layouts: 9.03 us -> 2.06 us
    pallas_call x1, Pallas kernels: 72.3 us -> 54.8 us  [on_device(): pl.pallas_call(kernel, out_shape=jax.ShapeDtypeStruct((1, 1, POS, HEADS *...]
    unnamed x19 -> x1, local copies, waits for them, and re-layouts: 9.03 us -> 2.06 us
where the time goes in v2:
time: 57.2 us; the launch traced here: 56.9 us
  Pallas kernels  54.8 us (96%)
  local copies, waits for them, and re-layouts  2.06 us (4%)
    pallas_call x1, Pallas kernels, on_device(): pl.pallas_call(kernel, out_shape=jax.ShapeDtypeStruct((1, 1, POS, HEADS *...  54.8 us
    unnamed x1, local copies, waits for them, and re-layouts  2.06 us

profile of v2, /device:TPU:0, one launch (start us, length us, event | category | flops | bytes accessed | tf_op | source)
XLA Modules:
  0.0 56.9 jit_solution(15435916766789902427)
XLA Ops:
  0.0 54.8 %attend.1 = bf16[1,1,256,1536]{3,2,1,0:T(8,128)(2,1)} custom-call(s32[8]{0:T(128)} %plan_hbm.1, s32[16]{0:T(128)} %frames_hbm.1, s32[16]{0:T(128)} %height_hbm.1, s32[16]{0:T(128)} %width_hbm.1, bf16[16,16,12,2,128]{4,3,2,1,0:T(2,128)(2,1)} %bitcast.11, bf16[16,16,12,2,128]{4,3,2,1,0:T(2,128)(2,1)} %bitcast.12, bf16[16,16,12,2,128]{4,3,2,1,0:T(2,128)(2,1)} %bitcast.13, ...), custom_call_target="tpu_custom_call" | custom-call | tf_op jit(solution)/shard_map/attend/pallas_call | solution.py:273
  54.8 2.1 %copy.11 = bf16[1,1,256,1536]{3,2,1,0:T(8,128)(2,1)} copy(bf16[1,1,256,1536]{3,2,1,0:T(8,128)(2,1)} %attend.1) | data formatting | bytes 1572864

commit v3 on v2

v3 whole, which is shorter than its diff:
```python
import functools
import math

import jax
import jax.numpy as jnp
from jax import lax
from jax.experimental import pallas as pl
from jax.experimental.pallas import tpu as pltpu
from jax.sharding import PartitionSpec as P

MESH = pl.DeviceIdType.MESH
D = 128
HEADS = 12
FRAMES = 16
POS = 256
DEVS = 128
HALF = FRAMES // 2
BLOCK = 16
PC = 128
VMEM_BYTES = 56 << 20
SU = 8
SCALE2 = D**-0.5 * math.log2(math.e)


def unit_of(z, c, x, y):
    whole = x * 4 + y
    over = jnp.where(whole >= HEADS, 1, 0)
    group = jnp.where(c == 0, 2 * z + over, 2 * z + 1)
    head = jnp.where(c == 0, whole - HEADS * over, 4 + 2 * x + lax.div(y, 2))
    first_frame = jnp.where(c == 0, 0, HALF * lax.rem(y, 2))
    return group, head, first_frame


def kernel(
    plan_hbm, frames_hbm, height_hbm, width_hbm, q_hbm, k_hbm, v_hbm, gq_hbm, gk_hbm, out,
    plan, frames, height, width, gq, gk, xq, xk, xv, stage, recv, spat, sendbuf, pair_bias,
    x_sem, in_send, in_recv, pair_send, pair_recv, out_send, out_recv, ready, mate,
):
    my_g = lax.axis_index("grp")
    my_s = lax.axis_index("sp")
    me = my_g * 16 + my_s
    mz, mc = lax.div(my_g, 2), lax.rem(my_g, 2)
    mx, my = lax.div(my_s, 4), lax.rem(my_s, 4)
    my_unit, my_head, my_first = unit_of(mz, mc, mx, my)

    barrier = pltpu.get_barrier_semaphore()
    loads = [
        pltpu.make_async_copy(ref, held, x_sem.at[t])
        for t, (ref, held) in enumerate((
            (plan_hbm, plan), (q_hbm, xq), (k_hbm, xk), (v_hbm, xv), (frames_hbm, frames),
            (height_hbm, height), (width_hbm, width), (gq_hbm, gq), (gk_hbm, gk),
        ))
    ]

    def greet_grp(i, _):
        pl.semaphore_signal(barrier, 1, device_id=(lax.rem(my_g + i, 8), my_s), device_id_type=MESH)
        return 0

    def greet_sp(i, _):
        pl.semaphore_signal(barrier, 1, device_id=(my_g, lax.rem(my_s + i, 16)), device_id_type=MESH)
        return 0

    def greet_all(i, _):
        pl.semaphore_signal(ready, 1, device_id=(lax.rem(my_g + i, 8), my_s), device_id_type=MESH)
        return 0

    for copy in loads[:4]:
        copy.start()
    lax.fori_loop(1, 16, greet_sp, 0)
    lax.fori_loop(1, 8, greet_grp, 0)
    for copy in loads[4:]:
        copy.start()

    def wait_bytes(ref, sem):
        pltpu.make_async_copy(ref, ref, sem).wait()

    def sent(part, to_core):
        def of(count):
            wait_bytes(recv.at[:, pl.ds(0, HALF), pl.ds(0, count)], in_send.at[part])

        @pl.when(mc == to_core)
        def _():
            of(DEVS // 2 - 1)

        @pl.when(mc != to_core)
        def _():
            of(DEVS // 2)

    stage_rows = stage.reshape(8, 3, FRAMES * HEADS * 2, D)

    def pick(t, held, z):
        x_rows = held.reshape(16, FRAMES * HEADS * 2, D)
        for c in range(2):
            stage_rows[2 * z + c, t] = x_rows[plan[2 * z + c]]

    def send(src, dst, sem, arrival, z, c, x, y):
        here = (z == mz) & (c == mc) & (x == mx) & (y == my)

        @pl.when(jnp.logical_not(here))
        def _():
            pltpu.make_async_remote_copy(
                src, dst, in_send.at[sem], in_recv.at[arrival],
                device_id=(2 * z + c, 4 * x + y), device_id_type=MESH,
            ).start()

        @pl.when(here)
        def _():
            pltpu.make_async_copy(src, dst, in_recv.at[arrival]).start()

    def send_half(z, x, y):
        group, head, first = unit_of(z, 1, x, y)
        send(
            stage.at[group, :, pl.ds(first, HALF), head], recv.at[:, pl.ds(0, HALF), me], 0, 0, z, 1, x, y
        )

    def send_part(part, z, x, y):
        group, head, _ = unit_of(z, 0, x, y)
        span = pl.ds(part * HALF, HALF)
        send(stage.at[group, :, span, head], recv.at[:, span, me], 1 + part, part, z, 0, x, y)

    def near(i):
        return mz, lax.rem(mx + lax.div(i, 4), 4), lax.rem(my + lax.rem(i, 4), 4)

    def plane(c):
        @pl.when(c == 1)
        def _():
            def body(i, _):
                send_half(*near(lax.rem(i * 5, 16)))
                return 0

            lax.fori_loop(0, 16, body, 0)

        @pl.when(c == 0)
        def _():
            def body(i, _):
                pass
                return 0

            lax.fori_loop(0, 16, body, 0)

    def column(i, _):
        z = lax.rem(mz + i, 4)
        send_half(z, mx, my)
        return 0

    def far(i, start):
        j = lax.rem(i * 7 + 22 * mc + start, 45)
        d = 1 + lax.div(j, 3)
        return lax.rem(mz + 1 + lax.rem(j, 3), 4), lax.rem(mx + lax.div(d, 4), 4), lax.rem(my + lax.rem(d, 4), 4)

    pl.semaphore_wait(barrier, 22)
    pl.semaphore_signal(mate, 1, device_id=(my_g + 1 - 2 * mc, my_s), device_id_type=MESH)
    lax.fori_loop(1, 8, greet_all, 0)
    loads[0].wait()
    for t, held in enumerate((xq, xk, xv)):
        loads[1 + t].wait()
        pick(t, held, mz)
    plane(mc)
    pl.semaphore_wait(mate, 1)
    plane(1 - mc)

    def pick_others(i, _):
        for t, held in enumerate((xq, xk, xv)):
            pick(t, held, lax.rem(mz + i, 4))
        return 0

    lax.fori_loop(1, 4, pick_others, 0)
    lax.fori_loop(1, 4, column, 0)
    pl.semaphore_wait(ready, 7)

    def far_half(i, _):
        send_half(*far(i, 0))
        return 0

    def first(i, _):
        send_part(0, *anywhere(i))
        return 0

    def second(i, _):
        send_part(1, *anywhere(i))
        return 0

    def anywhere(i):
        j = lax.rem(i * 29 + 32 * mc, 64)
        return lax.rem(mz + lax.rem(j, 4), 4), lax.rem(mx + lax.rem(lax.div(j, 4), 4), 4), lax.rem(my + lax.div(j, 16), 4)

    lax.fori_loop(0, 45, far_half, 0)
    lax.fori_loop(0, 64, first, 0)
    lax.fori_loop(0, 64, second, 0)
    for copy in loads[4:]:
        copy.wait()

    clip = plan[my_unit]
    live_frames = frames[clip]
    live_pos = height[clip] * width[clip]
    rows = recv.reshape(3, FRAMES, POS, D)
    key_bias = jnp.where(lax.broadcasted_iota(jnp.int32, (1, POS), 1) < live_pos, 0.0, -jnp.inf)

    def attend(q, i, live):
        scores = lax.dot_general(q, rows[1, i], (((1,), (1,)), ((), ())), preferred_element_type=jnp.float32)
        scores = scores + key_bias
        top = jnp.max(scores, axis=-1, keepdims=True)
        weights = jnp.exp2((scores - top) * SCALE2)
        total = jnp.sum(weights, axis=-1, keepdims=True)
        mixed = jnp.dot(weights.astype(jnp.bfloat16), rows[2, i], preferred_element_type=jnp.float32)
        on = jnp.where(my_first + i < live_frames, 1.0, 0.0)
        return (mixed * (live * on / total)).astype(jnp.bfloat16)

    gain = (gq[...] * gk[...]) * SCALE2
    T = FRAMES * BLOCK
    r_id = lax.broadcasted_iota(jnp.int32, (T, T), 0)
    c_id = lax.broadcasted_iota(jnp.int32, (T, T), 1)
    pair_on = (lax.rem(r_id, BLOCK) == lax.rem(c_id, BLOCK)) & (lax.div(c_id, BLOCK) < live_frames)
    pair_bias[...] = jnp.where(pair_on, 0.0, -jnp.inf)
    t_on = lax.div(lax.broadcasted_iota(jnp.int32, (T, 1), 0), BLOCK) < live_frames
    frame_on = jnp.where(t_on, 1.0, 0.0)

    def temporal(p0):
        xb = spat[:, pl.ds(p0, BLOCK), :].reshape(T, D)
        x = xb.astype(jnp.float32)
        inv = lax.rsqrt(jnp.sum(x * x, axis=-1, keepdims=True) * (1.0 / D) + 1e-6)
        y = x * inv * gain
        hi = y.astype(jnp.bfloat16)
        lo = (y - hi.astype(jnp.float32)).astype(jnp.bfloat16)
        scores = lax.dot_general(
            jnp.concatenate([xb, xb], axis=1), jnp.concatenate([hi, lo], axis=1),
            (((1,), (1,)), ((), ())), preferred_element_type=jnp.float32,
        )
        scores = scores + pair_bias[...]
        top = jnp.max(scores, axis=-1, keepdims=True)
        weights = jnp.exp2((scores - top) * inv)
        total = jnp.sum(weights, axis=-1, keepdims=True)
        mixed = jnp.dot(weights.astype(jnp.bfloat16), xb, preferred_element_type=jnp.float32)
        mixed = (mixed * (frame_on / total)).astype(jnp.bfloat16).astype(jnp.float32)
        sendbuf[:, pl.ds(p0, BLOCK), :] = (x + mixed).astype(jnp.bfloat16).reshape(FRAMES, BLOCK, D)

    head_lanes = pl.ds(pl.multiple_of(my_head * D, D), D)
    own_unit = my_unit == my_g

    def chunk(p0):
        for k in range(PC // BLOCK):
            temporal(p0 + k * BLOCK)
        span = pl.ds(p0, PC)

        def send_frame(i, _):
            f = lax.rem(my_s + i, 16)
            src, dst = sendbuf.at[f, span], out.at[0, 0, span, head_lanes]
            here = (i == 0) & own_unit

            @pl.when(jnp.logical_not(here))
            def _():
                pltpu.make_async_remote_copy(
                    src, dst, out_send, out_recv, device_id=(my_unit, f), device_id_type=MESH
                ).start()

            @pl.when(here)
            def _():
                pltpu.make_async_copy(src, dst, out_recv).start()

            return 0

        lax.fori_loop(0, 16, send_frame, 0)

    @pl.when(mc == 1)
    def _():
        wait_bytes(recv.at[:, pl.ds(0, HALF)], in_recv.at[0])
        live = jnp.where(lax.broadcasted_iota(jnp.int32, (POS, 1), 0) < live_pos, 1.0, 0.0)

        def group(b, _):
            for k in range(SU):
                i = b * SU + k
                spat[my_first + i] = attend(rows[0, i], i, live)
            return 0

        lax.fori_loop(0, HALF // SU, group, 0)

        half = lax.rem(my, 2)
        theirs = pl.ds(pl.multiple_of((1 - half) * (POS // 2), POS // 2), POS // 2)
        block = spat.at[pl.ds(my_first, HALF), theirs]
        copy = pltpu.make_async_remote_copy(
            block, block, pair_send, pair_recv, device_id=(my_g, my_s + 1 - 2 * half), device_id_type=MESH
        )
        copy.start()
        copy.wait()

        def half_chunk(k, _):
            chunk(pl.multiple_of(half * (POS // 2) + k * PC, PC))
            return 0

        lax.fori_loop(0, POS // 2 // PC, half_chunk, 0)
        wait_bytes(sendbuf.at[pl.ds(0, 15), pl.ds(0, POS // 2)], out_send)

    @pl.when(mc == 0)
    def _():
        live = jnp.where(lax.broadcasted_iota(jnp.int32, (POS, 1), 0) < live_pos, 1.0, 0.0)

        def part(k, _):
            wait_bytes(recv.at[:, pl.ds(0, HALF)], in_recv.at[k])

            def group(b, _):
                for u in range(SU):
                    i = k * HALF + b * SU + u
                    spat[i] = attend(rows[0, i], i, live)
                return 0

            lax.fori_loop(0, HALF // SU, group, 0)
            return 0

        lax.fori_loop(0, 2, part, 0)

        def all_chunks(k, _):
            chunk(pl.multiple_of(k * PC, PC))
            return 0

        lax.fori_loop(0, POS // PC, all_chunks, 0)

        @pl.when(own_unit)
        def _():
            wait_bytes(sendbuf.at[pl.ds(0, 15)], out_send)

        @pl.when(jnp.logical_not(own_unit))
        def _():
            wait_bytes(sendbuf, out_send)

    sent(0, 1)
    sent(1, 0)
    sent(2, 0)
    wait_bytes(out, out_recv)


def on_device(
    queries, key_rows, values, query_gain, key_gain, frames_per_clip, latent_height, latent_width, clip_plan
):
    def by_head(x):
        return x.reshape(16, FRAMES, 2, HEADS, D).transpose(0, 1, 3, 2, 4)

    hbm = pl.BlockSpec(memory_space=pl.ANY)
    clips = pltpu.VMEM((16, FRAMES, HEADS, 2, D), jnp.bfloat16)
    counts = pltpu.SMEM((16,), jnp.int32)
    dma = pltpu.SemaphoreType.DMA
    return pl.pallas_call(
        kernel,
        out_shape=pltpu.VMEM((1, 1, POS, HEADS * D), jnp.bfloat16),
        in_specs=[hbm] * 9,
        out_specs=hbm,
        scratch_shapes=[
            pltpu.SMEM((8,), jnp.int32), counts, counts, counts,
            pltpu.VMEM((1, D), jnp.float32), pltpu.VMEM((1, D), jnp.float32),
            clips, clips, clips,
            pltpu.VMEM((8, 3, FRAMES, HEADS, 2, D), jnp.bfloat16),
            pltpu.VMEM((3, FRAMES, DEVS, 2, D), jnp.bfloat16),
            pltpu.VMEM((FRAMES, POS, D), jnp.bfloat16),
            pltpu.VMEM((FRAMES, POS, D), jnp.bfloat16),
            pltpu.VMEM((FRAMES * BLOCK, FRAMES * BLOCK), jnp.float32),
            dma((9,)), dma((3,)), dma((2,)), dma, dma, dma, dma,
            pltpu.SemaphoreType.REGULAR, pltpu.SemaphoreType.REGULAR,
        ],
        compiler_params=pltpu.CompilerParams(
            collective_id=0, has_side_effects=True, vmem_limit_bytes=VMEM_BYTES
        ),
        name="attend",
    )(
        clip_plan, frames_per_clip, latent_height, latent_width,
        by_head(queries), by_head(key_rows), by_head(values),
        query_gain.reshape(1, D), key_gain.reshape(1, D),
    )


def solution(mesh):
    split = P(None, None, ("grp", "sp"), None)
    return jax.shard_map(
        on_device,
        mesh=mesh,
        in_specs=(split, split, split, P(), P(), P(), P(), P(), P()),
        out_specs=P("grp", "sp", None, None),
        check_vma=False,
    )
```

time: 57.2 us -> 52.4 us (0.916)
  Pallas kernels: 54.8 us -> 51.4 us
  local copies, waits for them, and re-layouts: 2.06 us -> 0.88 us
    pallas_call x1, Pallas kernels: 54.8 us -> 51.4 us  [on_device(): pl.pallas_call(kernel, out_shape=pltpu.VMEM((1, 1, POS, HEADS * D), jnp.b...]
    unnamed x1, local copies, waits for them, and re-layouts: 2.06 us -> 0.88 us
where the time goes in v3:
time: 52.4 us; the launch traced here: 52.3 us
  Pallas kernels  51.4 us (98%)
  local copies, waits for them, and re-layouts  0.88 us (2%)
    pallas_call x1, Pallas kernels, on_device(): pl.pallas_call(kernel, out_shape=pltpu.VMEM((1, 1, POS, HEADS * D), jnp.b...  51.4 us

profile of v3, /device:TPU:0, one launch (start us, length us, event | category | flops | bytes accessed | tf_op | source)
XLA Modules:
  0.0 52.3 jit_solution(2122703570443051872)
XLA Ops:
  0.0 51.4 %attend.1 = bf16[1,1,256,1536]{3,2,1,0:T(8,128)(2,1)S(1)} custom-call(s32[8]{0:T(128)} %plan_hbm.1, s32[16]{0:T(128)} %frames_hbm.1, s32[16]{0:T(128)} %height_hbm.1, s32[16]{0:T(128)} %width_hbm.1, bf16[16,16,12,2,128]{4,3,2,1,0:T(2,128)(2,1)} %bitcast.11, bf16[16,16,12,2,128]{4,3,2,1,0:T(2,128)(2,1)} %bitcast.12, bf16[16,16,12,2,128]{4,3,2,1,0:T(2,128)(2,1)} %bitcast.13, ...), custom_call_target="tpu_custom_call" | custom-call | tf_op jit(solution)/shard_map/attend/pallas_call | solution.py:341
  51.4 0.9 %copy.11 = bf16[1,1,256,1536]{3,2,1,0:T(8,128)(2,1)} copy(bf16[1,1,256,1536]{3,2,1,0:T(8,128)(2,1)S(1)} %attend.1) | data formatting | bytes 1572864

commit v4 on v3

--- a/solution.py
+++ b/solution.py
@@ -19,6 +19,8 @@
 PC = 128
 VMEM_BYTES = 56 << 20
 SU = 8
+LU = 8
+TU = 8
 SCALE2 = D**-0.5 * math.log2(math.e)
 
 
@@ -143,11 +145,6 @@
         send_half(z, mx, my)
         return 0
 
-    def far(i, start):
-        j = lax.rem(i * 7 + 22 * mc + start, 45)
-        d = 1 + lax.div(j, 3)
-        return lax.rem(mz + 1 + lax.rem(j, 3), 4), lax.rem(mx + lax.div(d, 4), 4), lax.rem(my + lax.rem(d, 4), 4)
-
     pl.semaphore_wait(barrier, 22)
     pl.semaphore_signal(mate, 1, device_id=(my_g + 1 - 2 * mc, my_s), device_id_type=MESH)
     lax.fori_loop(1, 8, greet_all, 0)
@@ -169,7 +166,12 @@
     pl.semaphore_wait(ready, 7)
 
     def far_half(i, _):
-        send_half(*far(i, 0))
+        z, x, y = anywhere(i)
+
+        @pl.when((z != mz) & ((x != mx) | (y != my)))
+        def _():
+            send_half(z, x, y)
+
         return 0
 
     def first(i, _):
@@ -184,7 +186,7 @@
         j = lax.rem(i * 29 + 32 * mc, 64)
         return lax.rem(mz + lax.rem(j, 4), 4), lax.rem(mx + lax.rem(lax.div(j, 4), 4), 4), lax.rem(my + lax.div(j, 16), 4)
 
-    lax.fori_loop(0, 45, far_half, 0)
+    lax.fori_loop(0, 64, far_half, 0)
     lax.fori_loop(0, 64, first, 0)
     lax.fori_loop(0, 64, second, 0)
     for copy in loads[4:]:
@@ -238,8 +240,12 @@
     own_unit = my_unit == my_g
 
     def chunk(p0):
-        for k in range(PC // BLOCK):
-            temporal(p0 + k * BLOCK)
+        def blocks(b, _):
+            for k in range(TU):
+                temporal(pl.multiple_of(p0 + (b * TU + k) * BLOCK, BLOCK))
+            return 0
+
+        lax.fori_loop(0, PC // BLOCK // TU, blocks, 0)
         span = pl.ds(p0, PC)
 
         def send_frame(i, _):
@@ -293,26 +299,35 @@
     @pl.when(mc == 0)
     def _():
         live = jnp.where(lax.broadcasted_iota(jnp.int32, (POS, 1), 0) < live_pos, 1.0, 0.0)
-
-        def part(k, _):
-            wait_bytes(recv.at[:, pl.ds(0, HALF)], in_recv.at[k])
-
-            def group(b, _):
-                for u in range(SU):
-                    i = k * HALF + b * SU + u
-                    spat[i] = attend(rows[0, i], i, live)
+        wait_bytes(recv.at[:, pl.ds(0, HALF)], in_recv.at[0])
+
+        def first_frames(b, _):
+            for k in range(SU):
+                i = b * SU + k
+                spat[i] = attend(rows[0, i], i, live)
+            return 0
+
+        lax.fori_loop(0, HALF // SU, first_frames, 0)
+
+        wait_bytes(recv.at[:, pl.ds(0, HALF)], in_recv.at[1])
+
+        def finish(c, _):
+            p0 = pl.multiple_of(c * PC, PC)
+            span = pl.ds(p0, PC)
+            place = p0 + lax.broadcasted_iota(jnp.int32, (PC, 1), 0)
+            on = jnp.where(place < live_pos, 1.0, 0.0)
+
+            def last_frames(b, _):
+                for k in range(LU):
+                    i = HALF + b * LU + k
+                    spat[i, span] = attend(rows[0, i, span], i, on)
                 return 0
 
-            lax.fori_loop(0, HALF // SU, group, 0)
-            return 0
-
-        lax.fori_loop(0, 2, part, 0)
-
-        def all_chunks(k, _):
-            chunk(pl.multiple_of(k * PC, PC))
-            return 0
-
-        lax.fori_loop(0, POS // PC, all_chunks, 0)
+            lax.fori_loop(0, HALF // LU, last_frames, 0)
+            chunk(p0)
+            return 0
+
+        lax.fori_loop(0, POS // PC, finish, 0)
 
         @pl.when(own_unit)
         def _():

time: 52.4 us -> 51.8 us (0.989)
  Pallas kernels: 51.4 us -> 50.8 us
    pallas_call x1, Pallas kernels: 51.4 us -> 50.8 us  [on_device(): pl.pallas_call(kernel, out_shape=pltpu.VMEM((1, 1, POS, HEADS * D), jnp.b...]
where the time goes in v4:
time: 51.8 us; the launch traced here: 51.7 us
  Pallas kernels  50.8 us (98%)
  local copies, waits for them, and re-layouts  0.88 us (2%)
    pallas_call x1, Pallas kernels, on_device(): pl.pallas_call(kernel, out_shape=pltpu.VMEM((1, 1, POS, HEADS * D), jnp.b...  50.8 us

profile of v4, /device:TPU:0, one launch (start us, length us, event | category | flops | bytes accessed | tf_op | source)
XLA Modules:
  0.0 51.7 jit_solution(16380638727563245919)
XLA Ops:
  0.0 50.8 %attend.1 = bf16[1,1,256,1536]{3,2,1,0:T(8,128)(2,1)S(1)} custom-call(s32[8]{0:T(128)} %plan_hbm.1, s32[16]{0:T(128)} %frames_hbm.1, s32[16]{0:T(128)} %height_hbm.1, s32[16]{0:T(128)} %width_hbm.1, bf16[16,16,12,2,128]{4,3,2,1,0:T(2,128)(2,1)} %bitcast.11, bf16[16,16,12,2,128]{4,3,2,1,0:T(2,128)(2,1)} %bitcast.12, bf16[16,16,12,2,128]{4,3,2,1,0:T(2,128)(2,1)} %bitcast.13, ...), custom_call_target="tpu_custom_call" | custom-call | tf_op jit(solution)/shard_map/attend/pallas_call | solution.py:356
  50.8 0.9 %copy.11 = bf16[1,1,256,1536]{3,2,1,0:T(8,128)(2,1)} copy(bf16[1,1,256,1536]{3,2,1,0:T(8,128)(2,1)S(1)} %attend.1) | data formatting | bytes 1572864

commit v5 on v4

--- a/solution.py
+++ b/solution.py
@@ -19,6 +19,7 @@
 PC = 128
 VMEM_BYTES = 56 << 20
 SU = 8
+TIERS = ((0, 1, 3, 4, 12, 2, 8, 5), (7, 13, 15, 6, 9, 11, 14, 10))
 LU = 8
 TU = 8
 SCALE2 = D**-0.5 * math.log2(math.e)
@@ -198,13 +199,18 @@
     rows = recv.reshape(3, FRAMES, POS, D)
     key_bias = jnp.where(lax.broadcasted_iota(jnp.int32, (1, POS), 1) < live_pos, 0.0, -jnp.inf)
 
+    ones = jnp.ones((POS, D), jnp.bfloat16)
+
     def attend(q, i, live):
         scores = lax.dot_general(q, rows[1, i], (((1,), (1,)), ((), ())), preferred_element_type=jnp.float32)
         scores = scores + key_bias
         top = jnp.max(scores, axis=-1, keepdims=True)
         weights = jnp.exp2((scores - top) * SCALE2)
-        total = jnp.sum(weights, axis=-1, keepdims=True)
-        mixed = jnp.dot(weights.astype(jnp.bfloat16), rows[2, i], preferred_element_type=jnp.float32)
+        both = jnp.dot(
+            weights.astype(jnp.bfloat16), jnp.concatenate([rows[2, i], ones], axis=1),
+            preferred_element_type=jnp.float32,
+        )
+        mixed, total = both[:, :D], both[:, D:]
         on = jnp.where(my_first + i < live_frames, 1.0, 0.0)
         return (mixed * (live * on / total)).astype(jnp.bfloat16)
 
@@ -248,10 +254,9 @@
         lax.fori_loop(0, PC // BLOCK // TU, blocks, 0)
         span = pl.ds(p0, PC)
 
-        def send_frame(i, _):
-            f = lax.rem(my_s + i, 16)
+        def send_frame(f):
             src, dst = sendbuf.at[f, span], out.at[0, 0, span, head_lanes]
-            here = (i == 0) & own_unit
+            here = (f == my_s) & own_unit
 
             @pl.when(jnp.logical_not(here))
             def _():
@@ -263,9 +268,17 @@
             def _():
                 pltpu.make_async_copy(src, dst, out_recv).start()
 
-            return 0
-
-        lax.fori_loop(0, 16, send_frame, 0)
+        for tier in TIERS:
+
+            def send_tier(i, _, tier=tier):
+                k = lax.rem(my_s + i, len(tier))
+                f = tier[0]
+                for n, frame in enumerate(tier):
+                    f = jnp.where(k == n, frame, f)
+                send_frame(f)
+                return 0
+
+            lax.fori_loop(0, len(tier), send_tier, 0)
 
     @pl.when(mc == 1)
     def _():

time: 51.8 us -> 51.6 us (level)
  Pallas kernels: 50.8 us -> 50.1 us
    pallas_call x1, Pallas kernels: 50.8 us -> 50.1 us  [on_device(): pl.pallas_call(kernel, out_shape=pltpu.VMEM((1, 1, POS, HEADS * D), jnp.b...]
where the time goes in v5:
time: 51.6 us; the launch traced here: 51 us
  Pallas kernels  50.1 us (97%)
  local copies, waits for them, and re-layouts  0.88 us (2%)
    pallas_call x1, Pallas kernels, on_device(): pl.pallas_call(kernel, out_shape=pltpu.VMEM((1, 1, POS, HEADS * D), jnp.b...  50.1 us

profile of v5, /device:TPU:0, one launch (start us, length us, event | category | flops | bytes accessed | tf_op | source)
XLA Modules:
  0.0 51.0 jit_solution(14522537775731836362)
XLA Ops:
  0.0 50.1 %attend.1 = bf16[1,1,256,1536]{3,2,1,0:T(8,128)(2,1)S(1)} custom-call(s32[8]{0:T(128)} %plan_hbm.1, s32[16]{0:T(128)} %frames_hbm.1, s32[16]{0:T(128)} %height_hbm.1, s32[16]{0:T(128)} %width_hbm.1, bf16[16,16,12,2,128]{4,3,2,1,0:T(2,128)(2,1)} %bitcast.11, bf16[16,16,12,2,128]{4,3,2,1,0:T(2,128)(2,1)} %bitcast.12, bf16[16,16,12,2,128]{4,3,2,1,0:T(2,128)(2,1)} %bitcast.13, ...), custom_call_target="tpu_custom_call" | custom-call | tf_op jit(solution)/shard_map/attend/pallas_call | solution.py:369
  50.1 0.9 %copy.11 = bf16[1,1,256,1536]{3,2,1,0:T(8,128)(2,1)} copy(bf16[1,1,256,1536]{3,2,1,0:T(8,128)(2,1)S(1)} %attend.1) | data formatting | bytes 1572864

commit v6 on v5

--- a/solution.py
+++ b/solution.py
@@ -237,9 +237,11 @@
         scores = scores + pair_bias[...]
         top = jnp.max(scores, axis=-1, keepdims=True)
         weights = jnp.exp2((scores - top) * inv)
-        total = jnp.sum(weights, axis=-1, keepdims=True)
-        mixed = jnp.dot(weights.astype(jnp.bfloat16), xb, preferred_element_type=jnp.float32)
-        mixed = (mixed * (frame_on / total)).astype(jnp.bfloat16).astype(jnp.float32)
+        both = jnp.dot(
+            weights.astype(jnp.bfloat16), jnp.concatenate([xb, ones], axis=1),
+            preferred_element_type=jnp.float32,
+        )
+        mixed = (both[:, :D] * (frame_on / both[:, D:])).astype(jnp.bfloat16).astype(jnp.float32)
         sendbuf[:, pl.ds(p0, BLOCK), :] = (x + mixed).astype(jnp.bfloat16).reshape(FRAMES, BLOCK, D)
 
     head_lanes = pl.ds(pl.multiple_of(my_head * D, D), D)

time: 51.6 us -> 51.6 us (level)
  no operation moved by 1% of the time
where the time goes in v6:
time: 51.6 us; the launch traced here: 51.1 us
  Pallas kernels  50.2 us (97%)
  local copies, waits for them, and re-layouts  0.88 us (2%)
    pallas_call x1, Pallas kernels, on_device(): pl.pallas_call(kernel, out_shape=pltpu.VMEM((1, 1, POS, HEADS * D), jnp.b...  50.2 us

profile of v6, /device:TPU:0, one launch (start us, length us, event | category | flops | bytes accessed | tf_op | source)
XLA Modules:
  0.0 51.1 jit_solution(11695258286379513610)
XLA Ops:
  0.0 50.2 %attend.1 = bf16[1,1,256,1536]{3,2,1,0:T(8,128)(2,1)S(1)} custom-call(s32[8]{0:T(128)} %plan_hbm.1, s32[16]{0:T(128)} %frames_hbm.1, s32[16]{0:T(128)} %height_hbm.1, s32[16]{0:T(128)} %width_hbm.1, bf16[16,16,12,2,128]{4,3,2,1,0:T(2,128)(2,1)} %bitcast.11, bf16[16,16,12,2,128]{4,3,2,1,0:T(2,128)(2,1)} %bitcast.12, bf16[16,16,12,2,128]{4,3,2,1,0:T(2,128)(2,1)} %bitcast.13, ...), custom_call_target="tpu_custom_call" | custom-call | tf_op jit(solution)/shard_map/attend/pallas_call | solution.py:371
  50.2 0.9 %copy.11 = bf16[1,1,256,1536]{3,2,1,0:T(8,128)(2,1)} copy(bf16[1,1,256,1536]{3,2,1,0:T(8,128)(2,1)S(1)} %attend.1) | data formatting | bytes 1572864
